TPU v7x, 1024 devices: a whole 8x8x8 slice. The times are simulated.
1024 devices in a mesh: vpair: 128 (over y, z, core), opair: 8 (over x).
Axes of the slice: x: 8, y: 8, z: 8, core: 2. Of those that a mesh axis runs over, the one named last changes fastest.
Arguments:
- amplitudes: bfloat16 [256, 512, 512], P('opair', 'vpair'), may hold values from -6 to 6
- integrals: bfloat16 [192, 32, 512, 512], P('opair', None, 'vpair'), may hold values from -0.3125 to 0.3125
- pair_list: int32 [256, 2], replicated, may hold values from 0 to 199, as said below
- slab_tiles: int32 [192], replicated, may hold values from 0 to 8191, as said below
- occ_irrep: int32 [200], replicated, may hold values from 0 to 7
- vir_irrep: int32 [512], replicated, may hold values from 0 to 7
- occ_energy: float32 [200], replicated, may hold values from -2 to -0.5
- vir_energy: float32 [512], replicated, may hold values from 0.1 to 2.5
Outputs:
- ladder: bfloat16 [256, 512, 512], P('opair', 'vpair')
Inputs may be any that keep to these rules, and one draw needn't show every extreme that they name: `pair_list`: each row is an ordered pair of distinct occupied orbitals; all rows differ, and for each row (i, j) the row (j, i) is present. `slab_tiles`: the tile ids are distinct. The owner of tile t is the index of vpair that holds virtual t // 16 among its 4; no owner has more than 3 tiles of the slab, and one owner has exactly 3.
All inputs are finite; a program needn't handle non-finite values.
Results may differ from a plain program's by a relative error of at most 0.0051.
Values may be sent and summed in bfloat16 or wider, within the bound.
A program may use at most 32 MiB of HBM per device.

v0:
```python
import jax
import jax.numpy as jnp
from jax import lax
from jax.sharding import PartitionSpec as P


def table_lookup(indices, table):
    hits = indices[..., None] == jnp.arange(table.shape[0], dtype=jnp.int32)
    return jnp.sum(jnp.where(hits, table, jnp.zeros((), table.dtype)), axis=-1)


def local(
    amplitudes, integrals, pair_list, slab_tiles, occ_irrep, vir_irrep, occ_energy, vir_energy
):
    vp_index = lax.axis_index("vpair")
    op_index = lax.axis_index("opair")
    op_dev, a_dev, virtuals = amplitudes.shape
    part_tiles = integrals.shape[0]
    tile_width = integrals.shape[1]
    pair_count = pair_list.shape[0]
    d_blocks = virtuals // tile_width
    local_tiles = a_dev * d_blocks
    first_occ = pair_list[:, 0]
    second_occ = pair_list[:, 1]
    swapped = lax.all_to_all(amplitudes, "vpair", split_axis=2, concat_axis=1, tiled=True)
    flipped = jnp.swapaxes(swapped, 1, 2)
    direct_tiles = amplitudes.reshape(op_dev, local_tiles, tile_width)
    flipped_tiles = flipped.reshape(op_dev, local_tiles, tile_width)
    c_index = slab_tiles // d_blocks
    is_owned = c_index // a_dev == vp_index
    local_index = (c_index - vp_index * a_dev) * d_blocks + slab_tiles % d_blocks
    tile_range = jnp.arange(local_tiles, dtype=jnp.int32)
    pick_hot = (is_owned[:, None] & (local_index[:, None] == tile_range[None, :])).astype(
        jnp.bfloat16
    )
    owned_direct = jnp.einsum(
        "kl,ple->pke", pick_hot, direct_tiles, preferred_element_type=jnp.float32
    )
    owned_flipped = jnp.einsum(
        "kl,ple->pke", pick_hot, flipped_tiles, preferred_element_type=jnp.float32
    )
    summed_direct, summed_flipped = lax.psum((owned_direct, owned_flipped), "vpair")
    slab_direct = summed_direct.astype(jnp.bfloat16)
    slab_flipped = summed_flipped.astype(jnp.bfloat16)
    part_direct, part_flipped = (
        lax.all_to_all(slab_direct, "opair", split_axis=1, concat_axis=0, tiled=True),
        lax.all_to_all(slab_flipped, "opair", split_axis=1, concat_axis=0, tiled=True),
    )
    mirror_hot = (
        (first_occ[None, :] == second_occ[:, None]) & (second_occ[None, :] == first_occ[:, None])
    ).astype(jnp.bfloat16)
    mirrored = jnp.einsum(
        "pq,qke->pke", mirror_hot, part_flipped, preferred_element_type=jnp.float32
    )
    pair_sym = jnp.bitwise_xor(
        table_lookup(first_occ, occ_irrep), table_lookup(second_occ, occ_irrep)
    )
    own_tiles = lax.dynamic_slice_in_dim(slab_tiles, op_index * part_tiles, part_tiles)
    c_irrep = table_lookup(own_tiles // d_blocks, vir_irrep)
    block_irrep = vir_irrep.reshape(d_blocks, tile_width)
    block_hits = (
        (own_tiles % d_blocks)[:, None] == jnp.arange(d_blocks, dtype=jnp.int32)[None, :]
    )[:, :, None]
    d_irrep = jnp.sum(jnp.where(block_hits, block_irrep[None], 0), axis=1)
    tile_sym = jnp.bitwise_xor(c_irrep[:, None], d_irrep)
    allowed = pair_sym[:, None, None] == tile_sym[None]
    summed = part_direct.astype(jnp.float32) + mirrored
    sym_amp = jnp.where(allowed, summed, jnp.float32(0.0)).astype(jnp.bfloat16)
    sym_rows = sym_amp.reshape(pair_count, part_tiles * tile_width)
    weights = integrals.reshape(part_tiles * tile_width, a_dev * virtuals)
    partial_sum = lax.psum_scatter(
        jnp.dot(sym_rows, weights, preferred_element_type=jnp.float32),
        "opair",
        scatter_dimension=0,
        tiled=True,
    )
    own_first = lax.dynamic_slice_in_dim(first_occ, op_index * op_dev, op_dev)
    own_second = lax.dynamic_slice_in_dim(second_occ, op_index * op_dev, op_dev)
    pair_energy = table_lookup(own_first, occ_energy) + table_lookup(own_second, occ_energy)
    own_virtual = lax.dynamic_slice_in_dim(vir_energy, vp_index * a_dev, a_dev)
    denominator = (
        pair_energy[:, None, None] - own_virtual[None, :, None] - vir_energy[None, None, :]
    )
    return (partial_sum.reshape(op_dev, a_dev, virtuals) / denominator).astype(jnp.bfloat16)


def solution(mesh):
    in_specs = (
        P("opair", "vpair", None),
        P("opair", None, "vpair", None),
        P(),
        P(),
        P(),
        P(),
        P(),
        P(),
    )
    out_specs = P("opair", "vpair", None)
    return jax.shard_map(local, mesh=mesh, in_specs=in_specs, out_specs=out_specs, check_vma=False)
```

profile of v0, /device:TPU:1, one launch (start us, length us, event | category | flops | bytes accessed | tf_op | source)
XLA Modules:
  0.0 656.1 jit_solution(12317557256472702959)
XLA Ops:
  6.5 1.3 copy.59
  7.9 1.0 reshape.122
  8.9 25.2 %all-to-all-start.1 = ((bf16[128,2,256]{2,1,0:T(2,128)(2,1)}), bf16[128,2,256]{2,1,0:T(2,128)(2,1)S(1)}, u32[]{:S(2)}, u32[]{:S(2)}) async-start(bf16[128,2,256]{2,1,0:T(2,128)(2,1)} %reshape.122), calls=%async_computation.1 | async-start | bytes 262144 | tf_op jit(solution)/shard_map/all_to_all | solution.py:25
  34.1 0.7 fusion.19
  34.8 0.7 fusion.18
  35.5 1.2 reshape.106
  36.8 0.2 copy.55
  37.0 0.3 fusion.12
  37.3 9.0 %all-to-all-done.1 = bf16[128,2,256]{2,1,0:T(2,128)(2,1)S(1)} async-done(((bf16[128,2,256]{2,1,0:T(2,128)(2,1)}), bf16[128,2,256]{2,1,0:T(2,128)(2,1)S(1)}, u32[]{:S(2)}, u32[]{:S(2)}) %all-to-all-start.1) | async-done | bytes 131104 | tf_op jit(solution)/shard_map/all_to_all | solution.py:25
  46.3 0.3 reshape.123
  46.7 0.4 copy.61
  47.1 0.8 copy.63
  47.9 0.3 fusion.10
  48.2 503.7 %all-reduce.2 = (bf16[32,192,32]{1,2,0:T(8,128)(2,1)S(1)}, bf16[32,192,32]{1,2,0:T(8,128)(2,1)S(1)}) all-reduce(f32[32,192,32]{1,2,0:T(8,128)S(1)} %bitcast.63, f32[32,192,32]{1,2,0:T(8,128)S(1)} %bitcast.64), channel_id=1, replica_groups=mesh['vpair'=128,'opair'=8] {'vpair'}, use_global_device_ids=true, to_apply=%region_4.5 | all-reduce | flops 393216 | bytes 2359296 | tf_op jit(solution)/shard_map/psum | solution.py:42
  552.0 1.4 copy.64
  553.4 2.2 reshape.124
  555.6 6.5 all-to-all-start.2
  562.1 0.1 broadcast_in_dim.79
  562.2 4.6 copy.71
  566.8 0.1 select_reduce_fusion
  566.9 0.6 xor.19
  567.5 0.1 and_select_fusion.4
  567.6 0.1 iota_compare_fusion.6
  567.7 1.4 copy.56
  569.1 2.2 reshape.120
  571.3 1.6 all-to-all-done.2
  572.9 5.0 all-to-all-start
  577.9 0.2 reduce-scatter.2.cloned.1.call-start
  578.2 0.2 select_reduce_fusion.3
  578.4 0.1 select_reduce_fusion.2
  578.6 0.8 reshape.125
  579.3 1.1 copy.66
  580.4 1.1 reshape.117
  581.5 2.0 fusion.1
  583.5 5.1 all-to-all-done
  588.7 0.8 reshape.121
  589.4 1.3 copy.57
  590.8 2.7 reshape.112
  593.5 3.7 copy.58
  597.2 1.7 reshape.111
  599.0 1.5 select_convert_fusion
  600.6 4.2 fusion.21
  604.9 0.1 dynamic-slice_bitcast_fusion
  604.9 0.2 select_reduce_fusion.4
  605.1 0.1 dynamic_slice.15
  605.3 42.1 %reduce-scatter.2.cloned.1.call-done = f32[32,2048]{1,0:T(8,128)} async-done(((f32[256,2048]{1,0:T(8,128)}), f32[32,2048]{1,0:T(8,128)}) %reduce-scatter.2.cloned.1.call-update) | async-done | bytes 262160 | tf_op jit(solution)/shard_map/reduce_scatter | solution.py:71
  647.4 1.1 reshape.110
  648.5 0.8 fusion
  (25 shorter events, 0.3 us)
Async XLA Ops:
  8.9 37.5 %all-to-all-start.1 = ((bf16[128,2,256]{2,1,0:T(2,128)(2,1)}), bf16[128,2,256]{2,1,0:T(2,128)(2,1)S(1)}, u32[]{:S(2)}, u32[]{:S(2)}) async-start(bf16[128,2,256]{2,1,0:T(2,128)(2,1)} %reshape.122), calls=%async_computation.1 | async-start | bytes 262144 | tf_op jit(solution)/shard_map/all_to_all | solution.py:25
  48.2 513.9 %copy-start.6 = (s32[256,2]{0,1:T(2,128)S(1)}, s32[256,2]{0,1:T(2,128)}, u32[]{:S(2)}) copy-start(s32[256,2]{0,1:T(2,128)} %param.10) | copy-start | bytes 6148
  48.2 513.9 %copy-start.2 = (s32[512]{0:T(512)S(1)}, s32[512]{0:T(512)}, u32[]{:S(2)}) copy-start(s32[512]{0:T(512)} %param.13) | copy-start | bytes 6148
  555.6 17.3 %all-to-all-start.2 = ((bf16[8,2,12288]{2,1,0:T(2,128)(2,1)}), bf16[8,2,12288]{2,1,0:T(2,128)(2,1)S(1)}, u32[]{:S(2)}, u32[]{:S(2)}) async-start(bf16[8,2,12288]{2,1,0:T(2,128)(2,1)} %reshape.124), calls=%async_computation.2 | async-start | bytes 786432 | tf_op jit(solution)/shard_map/all_to_all | solution.py:47
  562.1 4.7 copy-start
  562.2 4.6 copy-start.7
  562.2 5.3 copy-start.3
  572.9 15.8 %all-to-all-start = ((bf16[8,2,12288]{2,1,0:T(2,128)(2,1)}), bf16[8,2,12288]{2,1,0:T(2,128)(2,1)S(1)}, u32[]{:S(2)}, u32[]{:S(2)}) async-start(bf16[8,2,12288]{2,1,0:T(2,128)(2,1)} %reshape.120), calls=%async_computation | async-start | bytes 786432 | tf_op jit(solution)/shard_map/all_to_all | solution.py:46
  577.9 69.4 %reduce-scatter.2.cloned.1.call-start = ((), (), s32[]{:S(2)}) async-start(), calls=%async_computation.4 | async-start | bytes 2359296 | tf_op jit(solution)/shard_map/reduce_scatter | solution.py:71
  597.2 1.8 copy-start.4
  600.5 4.3 copy-start.1
  600.5 4.4 copy-start.8
  600.6 4.6 copy-start.5
Sparse Core Ops, SparseCore 0:
  605.0 42.3 reduce-scatter.1
where the time goes:
time: 660 us; the launch traced here: 656 us
  blocking collectives  504 us (76%)
  waiting for transfers between devices  57.9 us (9%)
  starting transfers between devices  37 us (6%)
  local copies, waits for them, and re-layouts  31.8 us (5%)
  between operations  13.7 us (2%)
  matrix products  6.83 us (1%)
    psum x1, blocking collectives, local(): lax.psum((owned_direct, owned_flipped), 'vpair')  504 us
    reduce_scatter x1, waiting for transfers between devices, local(): lax.psum_scatter(jnp.dot(sym_rows, weights, preferred_element_type=jnp.fl...  42.1 us
    all_to_all x1, starting transfers between devices, local(): lax.all_to_all(amplitudes, 'vpair', split_axis=2, concat_axis=1, tiled=True)  25.2 us
    unnamed x27, local copies, waits for them, and re-layouts  14.3 us
  transfers between devices with their start and end apart: 4, of which 4 were waited for; matrix products, arithmetic and copies ran while one was open for 3% of the time, Pallas kernels for 0%

commit v1 on v0

v1 whole, which is shorter than its diff:
```python
import jax
import jax.numpy as jnp
from jax import lax
from jax.experimental import pallas as pl
from jax.experimental.pallas import tpu as pltpu
from jax.sharding import PartitionSpec as P

MESH = pl.DeviceIdType.MESH
BF = jnp.bfloat16
F32 = jnp.float32
I32 = jnp.int32
N = 8
PAIRS, ROWS, PIECE = 256, 32, 16
TILES, PART, WIDTH = 192, 24, 32
A_DEV, VIRT = 4, 512
DEPTH = PART * WIDTH
COLS = A_DEV * VIRT


def iota(shape, axis):
    return lax.broadcasted_iota(I32, shape, axis)


def hot(mask):
    return jnp.where(mask, 1.0, 0.0).astype(BF)


def dot(a, b):
    return jnp.dot(a, b, preferred_element_type=F32)


def own_slots(tiles, owner):
    place = iota((1, TILES), 1).astype(F32)
    held = (tiles >> 6) == owner
    found, last = [], None
    for _ in range(3):
        open_ = held if last is None else held & (place > last)
        last = jnp.min(jnp.where(open_, place, 999.0), axis=1, keepdims=True)
        found.append(last)
    return found


def by_slot(values, shape, axis):
    slot = iota(shape, axis) >> 5
    return jnp.where(slot == 0, values[0], jnp.where(slot == 1, values[1], values[2]))


def kernel(
    amp, integ, slab, pairs, virr, oirr, out,
    vraw, vr, xs, xa, perm, spread, psb, tsym, xown, xoth, zs, zr, ys, yr, sy, pf, rs, rr,
    vsem, xsem, csem, zsem, ysem, gsem, hsem, rsem,
):
    v = lax.axis_index("vpair")
    x = lax.axis_index("opair")
    y, z, c = v // 16, (v // 2) % N, v % 2

    def at_x(d):
        return {"vpair": v, "opair": (x + d) % N}

    def at_y(d):
        return {"vpair": (((y + d) % N) * N + z) * 2 + c, "opair": x}

    def at_z(d):
        return {"vpair": (y * N + (z + d) % N) * 2 + c, "opair": x}

    other = {"vpair": (y * N + z) * 2 + (1 - c), "opair": x}
    steps = range(1, N)
    pending = []

    def send(src, dst, sems, i, device):
        copy = pltpu.make_async_remote_copy(
            src_ref=src, dst_ref=dst, send_sem=sems.at[0, i], recv_sem=sems.at[1, i],
            device_id=device, device_id_type=MESH,
        )
        copy.start()
        pending.append(copy)
        return copy

    load = pltpu.make_async_copy(integ, vraw, vsem)
    load.start()
    barrier = pltpu.get_barrier_semaphore()
    for device in [f(d) for f in (at_x, at_y, at_z) for d in steps] + [other]:
        pl.semaphore_signal(barrier, inc=1, device_id=device, device_id_type=MESH)

    tiles = slab[...]
    c_of, d_of = tiles >> 4, tiles & 15
    pick = hot(iota((VIRT, TILES), 0) == jnp.where(d_of == v // 8, c_of, -1))
    found = own_slots(tiles, v)
    place = iota((1, TILES), 1).astype(F32)
    ids = [
        jnp.sum(jnp.where(place == k, tiles.astype(F32), 0.0), axis=1, keepdims=True) for k in found
    ]
    tile = by_slot(ids, (1, 128), 1).astype(I32)
    wide = iota((1, 128), 1) & 31
    pick_own = hot(iota((VIRT, 128), 0) == (tile & 15) * WIDTH + wide)
    block = amp[...].reshape(ROWS * A_DEV, VIRT)
    lane = iota((1, N * 128), 1)
    target = jnp.where((lane & 31) < PART, (lane >> 7) * PART + (lane & 31), -1)
    place_in = hot(iota((TILES, N * 128), 0) == target)
    row = iota((ROWS * A_DEV, 1), 0) & 3
    columns = dot(dot(block, pick).astype(BF), place_in)
    columns = jnp.where(row == ((lane >> 5) & 3), columns, 0.0).astype(BF)
    held = jnp.where(row == ((tile >> 4) & 3), dot(block, pick_own), 0.0).astype(BF)
    fold = hot((iota((ROWS, ROWS * A_DEV), 1) >> 2) == iota((ROWS, ROWS * A_DEV), 0))
    columns = dot(fold, columns).astype(BF)
    held = dot(fold, held).astype(BF)
    for o in range(N):
        xs[o, :, 0:128] = held
        xs[o, :, 128:256] = columns[:, o * 128 : (o + 1) * 128]
    pl.semaphore_wait(barrier, 3 * (N - 1) + 1)

    to_x = [send(xs.at[(x + d) % N], xa.at[x], xsem, d, at_x(d)) for d in steps]
    xa[pl.ds(x, 1)] = xs[pl.ds(x, 1)]

    lists = pairs[...]
    first, second = lists[0:1, :], lists[1:2, :]
    code = first * 256 + second
    swapped = jnp.broadcast_to((second * 256 + first).astype(F32), (PAIRS, PAIRS)).T
    perm[...] = hot(swapped == code.astype(F32))
    part_lane = iota((1, DEPTH), 1)
    for h in range(2):
        holder = (y * N + z) * 2 + h
        slots = [k - (x * PART).astype(F32) for k in own_slots(tiles, holder)]
        r = iota((128, 1), 0)
        slot_at = by_slot(slots, (128, 1), 0).astype(I32)
        slot_at = jnp.where(r < 96, slot_at, -1)
        spread[h, 0:128] = hot(
            (slot_at == (part_lane >> 5)) & ((r & 31) == (part_lane & 31))
        )
        spread[h, 128:256] = hot(
            ((r & 31) == (part_lane >> 5))
            & ((holder % N) * A_DEV + (r >> 5) == (part_lane & 31))
        )
    irrep_hot = hot(iota((oirr.shape[1], PAIRS), 0) == first)
    irrep_hot2 = hot(iota((oirr.shape[1], PAIRS), 0) == second)
    occ = jnp.broadcast_to(oirr[...].astype(F32), (8, oirr.shape[1])).astype(BF)
    pair_sym = dot(occ, irrep_hot).astype(I32) ^ dot(occ, irrep_hot2).astype(I32)
    psb[...] = jnp.broadcast_to(pair_sym[0:1].astype(F32), (128, PAIRS)).T
    own_hot = hot(iota((TILES, DEPTH), 0) == x * PART + (part_lane >> 5))

    def own(row_values):
        wide_values = jnp.broadcast_to(row_values.astype(F32), (8, row_values.shape[1])).astype(BF)
        return dot(wide_values, own_hot)[0:1].astype(I32)

    c_row = own(c_of >> 2) * 4 + own(c_of & 3)
    d_row = own(d_of) * WIDTH + (part_lane & 31)
    vir = jnp.broadcast_to(virr[...].astype(F32), (8, VIRT)).astype(BF)
    tile_sym = [
        dot(vir, hot(iota((VIRT, DEPTH), 0) == rows))[0:1].astype(I32) for rows in (c_row, d_row)
    ]
    tsym[...] = jnp.broadcast_to((tile_sym[0] ^ tile_sym[1]).astype(F32), (8, DEPTH))

    ri, ci = iota((128, 128), 0), iota((128, 128), 1)
    regroup = hot(((ri >> 5) == (ci & 3)) & ((ri & 31) == (ci >> 2)))

    def relayout(k, _):
        rows = dot(regroup, vraw[k].reshape(WIDTH * A_DEV, VIRT)).astype(BF)
        at = pl.ds(pl.multiple_of(k * WIDTH, WIDTH), WIDTH)
        for a in range(A_DEV):
            vr[a, at, :] = rows[a * WIDTH : (a + 1) * WIDTH]
        return 0

    load.wait()
    lax.fori_loop(0, 8, relayout, 0)
    for copy in to_x:
        copy.wait_recv()

    mirrored = dot(perm[...], xa[:, :, 128:256].reshape(PAIRS, 128)).astype(BF)
    xown[:, :, 128:256] = mirrored.reshape(2, 128, 128)
    xown[:, :, 0:128] = xa[:, :, 0:128].reshape(2, 128, 128)
    to_core = send(xown.at[1 - c], xoth, csem, 0, other)
    dense = dot(xown[c], spread[c])
    to_core.wait_recv()
    dense += dot(xoth[...], spread[1 - c])
    zs[...] = dense.astype(BF).reshape(N, PIECE, DEPTH)
    to_z = [send(zs.at[(z + d) % N], zr.at[z], zsem, d, at_z(d)) for d in steps]
    zr[pl.ds(z, 1)] = zs[pl.ds(z, 1)]
    lax.fori_loop(8, 16, relayout, 0)
    for copy in to_z:
        copy.wait_recv()
    total = zr[0].astype(F32)
    for i in steps:
        total += zr[i].astype(F32)
    ys[...] = total.astype(BF)
    to_y = [send(ys, yr.at[y], ysem, d, at_y(d)) for d in steps]
    yr[pl.ds(y, 1)] = ys[...].reshape(1, PIECE, DEPTH)
    lax.fori_loop(16, 24, relayout, 0)
    for copy in to_y:
        copy.wait_recv()
    total = yr[0].astype(F32)
    for i in steps:
        total += yr[i].astype(F32)
    mine = c * N + z
    sym_of = psb[pl.ds(pl.multiple_of(mine * PIECE, PIECE), PIECE), :][:, 0:1]
    total = jnp.where(sym_of == tsym[0:1, :], total, 0.0)
    sy[pl.ds(mine, 1)] = total.astype(BF).reshape(1, PIECE, DEPTH)
    to_z = [send(sy.at[mine], sy.at[mine], gsem, d, at_z(d)) for d in steps]
    to_other = [send(sy.at[mine], sy.at[mine], hsem, 0, other)]
    for d in (1, 7, 2, 6, 3, 5, 4):
        to_z[d - 1].wait_recv()
        got = c * N + (z + N - d) % N
        to_other.append(send(sy.at[got], sy.at[got], hsem, d, other))
    for copy in to_other:
        copy.wait_recv()

    def multiply(blocks):
        rows = jnp.concatenate(
            [sy[pl.ds(((x + d) % N) * 2, 2)].reshape(ROWS, DEPTH) for d in blocks], axis=0
        )
        for a in range(A_DEV):
            sums = dot(rows, vr[a])
            for i, d in enumerate(blocks):
                pf[d, :, a * VIRT : (a + 1) * VIRT] = sums[i * ROWS : (i + 1) * ROWS]

    ring = {}

    def pass_on(way, i, got):
        distance = 4 - i if i < 4 else 7 - i
        d = distance if way == 0 else N - distance
        half = 0 if (way == 0) == (i < 4) else PIECE
        value = pf[d, half : half + PIECE, :]
        if got is not None:
            value += rr[way, got].astype(F32)
        rs[way, i] = value.astype(BF)
        ring[way, i] = send(rs.at[way, i], rr.at[way, i], rsem.at[way], i, at_x(1 if way == 0 else N - 1))

    multiply((4, 3, 5, 2))
    for i in (0, 4):
        for way in range(2):
            pass_on(way, i, None)
    multiply((6, 1, 7, 0))
    for i in (0, 4, 1, 5, 2):
        for way in range(2):
            ring[way, i].wait_recv()
            pass_on(way, i + 1, i)
    for i in (3, 6):
        for way in range(2):
            ring[way, i].wait_recv()
    halves = []
    for half, mine_, theirs in ((0, 3, 6), (PIECE, 6, 3)):
        halves.append(
            pf[0, half : half + PIECE, :] + rr[0, mine_].astype(F32) + rr[1, theirs].astype(F32)
        )
    out[0:PIECE, :] = halves[0]
    out[PIECE:ROWS, :] = halves[1]
    for copy in pending:
        copy.wait_send()


def table_lookup(indices, table):
    hits = indices[..., None] == jnp.arange(table.shape[0], dtype=jnp.int32)
    return jnp.sum(jnp.where(hits, table, jnp.zeros((), table.dtype)), axis=-1)


def local(
    amplitudes, integrals, pair_list, slab_tiles, occ_irrep, vir_irrep, occ_energy, vir_energy
):
    vp_index = lax.axis_index("vpair")
    op_index = lax.axis_index("opair")
    vmem = pl.BlockSpec(memory_space=pltpu.VMEM)
    dma = pltpu.SemaphoreType.DMA
    partial_sum = pl.pallas_call(
        kernel,
        out_shape=jax.ShapeDtypeStruct((ROWS, COLS), F32),
        in_specs=[vmem, pl.BlockSpec(memory_space=pl.ANY), vmem, vmem, vmem, vmem],
        out_specs=vmem,
        scratch_shapes=[
            pltpu.VMEM((PART, WIDTH, A_DEV, VIRT), BF),
            pltpu.VMEM((A_DEV, DEPTH, VIRT), BF),
            pltpu.VMEM((N, ROWS, 256), BF),
            pltpu.VMEM((N, ROWS, 256), BF),
            pltpu.VMEM((PAIRS, PAIRS), BF),
            pltpu.VMEM((2, 256, DEPTH), BF),
            pltpu.VMEM((PAIRS, 128), F32),
            pltpu.VMEM((8, DEPTH), F32),
            pltpu.VMEM((2, 128, 256), BF),
            pltpu.VMEM((128, 256), BF),
            pltpu.VMEM((N, PIECE, DEPTH), BF),
            pltpu.VMEM((N, PIECE, DEPTH), BF),
            pltpu.VMEM((PIECE, DEPTH), BF),
            pltpu.VMEM((N, PIECE, DEPTH), BF),
            pltpu.VMEM((2 * N, PIECE, DEPTH), BF),
            pltpu.VMEM((N, ROWS, COLS), F32),
            pltpu.VMEM((2, 7, PIECE, COLS), BF),
            pltpu.VMEM((2, 7, PIECE, COLS), BF),
            dma,
            dma((2, N)),
            dma((2, 1)),
            dma((2, N)),
            dma((2, N)),
            dma((2, N)),
            dma((2, N)),
            dma((2, 2, 7)),
        ],
        compiler_params=pltpu.CompilerParams(
            collective_id=0, has_side_effects=True, vmem_limit_bytes=60 << 20
        ),
    )(
        amplitudes,
        integrals,
        slab_tiles.reshape(1, TILES),
        pair_list.T,
        vir_irrep.reshape(1, VIRT),
        occ_irrep.reshape(1, -1),
    )
    own = lax.dynamic_slice_in_dim(pair_list, op_index * ROWS, ROWS)
    pair_energy = table_lookup(own[:, 0], occ_energy) + table_lookup(own[:, 1], occ_energy)
    own_virtual = lax.dynamic_slice_in_dim(vir_energy, vp_index * A_DEV, A_DEV)
    denominator = (
        pair_energy[:, None, None] - own_virtual[None, :, None] - vir_energy[None, None, :]
    )
    return (partial_sum.reshape(ROWS, A_DEV, VIRT) / denominator).astype(BF)


def solution(mesh):
    in_specs = (
        P("opair", "vpair", None), P("opair", None, "vpair", None), P(), P(), P(), P(), P(), P(),
    )
    out_specs = P("opair", "vpair", None)
    return jax.shard_map(local, mesh=mesh, in_specs=in_specs, out_specs=out_specs, check_vma=False)
```

time: 660 us -> 73 us (0.11)
  blocking collectives: 504 us -> 0 us
  Pallas kernels: 0 us -> 70.4 us
  waiting for transfers between devices: 57.9 us -> 0 us
  starting transfers between devices: 37 us -> 0 us
  local copies, waits for them, and re-layouts: 31.8 us -> 1.29 us
  between operations: 13.7 us -> 0.04 us
  matrix products: 6.83 us -> 0 us
    psum x1 -> x0, blocking collectives: 504 us -> none  [local(): lax.psum((owned_direct, owned_flipped), 'vpair')]
    pallas_call x0 -> x1, Pallas kernels: none -> 70.4 us  [local(): pl.pallas_call(kernel, out_shape=jax.ShapeDtypeStruct((ROWS, COLS), F32),...]
    reduce_scatter x1 -> x0, waiting for transfers between devices: 42.1 us -> none  [local(): lax.psum_scatter(jnp.dot(sym_rows, weights, preferred_element_type=jnp.fl...]
    all_to_all x3 -> x0, starting transfers between devices: 36.8 us -> none  [the longest x1 25.2 us: local(): lax.all_to_all(amplitudes, 'vpair', split_axis=2, concat_axis=1, tiled=True)]
    all_to_all x3 -> x0, waiting for transfers between devices: 15.8 us -> none  [the longest x1 9.05 us: local(): lax.all_to_all(amplitudes, 'vpair', split_axis=2, concat_axis=1, tiled=True)]
    unnamed x27 -> x6, local copies, waits for them, and re-layouts: 14.3 us -> 0.01 us
    convert_element_type x5 -> x0, local copies, waits for them, and re-layouts: 11 us -> none  [the longest x3 8.18 us: local(): summed = part_direct.astype(jnp.float32) + mirrored]
  transfers between devices with their start and end apart: 4 -> 0, of which waited for: 4 -> 0; matrix products, arithmetic and copies ran while one was open for 3% -> 0% of each run, Pallas kernels for 0% -> 0%
where the time goes in v1:
time: 73 us; the launch traced here: 72.8 us
  Pallas kernels  70.4 us (96%)
  local copies, waits for them, and re-layouts  1.29 us (2%)
  other arithmetic  1.06 us (1%)
    pallas_call x1, Pallas kernels, local(): pl.pallas_call(kernel, out_shape=jax.ShapeDtypeStruct((ROWS, COLS), F32),...  70.4 us

profile of v1, /device:TPU:1, one launch (start us, length us, event | category | flops | bytes accessed | tf_op | source)
XLA Modules:
  0.0 72.8 jit_solution(2677299564887675438)
XLA Ops:
  0.0 0.0 copy-start
  0.0 0.0 copy-start.1
  0.0 0.0 copy-start.2
  0.0 70.4 %shard_map.82 = f32[32,2048]{1,0:T(8,128)} custom-call(bf16[32,4,512]{2,1,0:T(4,128)(2,1)} %amp.1, bf16[24,32,4,512]{3,2,1,0:T(4,128)(2,1)} %integ.1, s32[1,192]{1,0:T(1,128)} %bitcast.10, s32[2,256]{1,0:T(2,128)} %bitcast.8, s32[1,512]{1,0:T(1,128)} %bitcast.9, s32[1,200]{1,0:T(1,128)} %bitcast.11), custom_call_target="tpu_custom_call" | custom-call | tf_op jit(solution)/shard_map/pallas_call | solution.py:262
  70.4 1.1 %reshape.52 = f32[32,4,512]{2,1,0:T(4,128)S(1)} reshape(f32[32,2048]{1,0:T(8,128)} %shard_map.82) | data formatting | bytes 524288 | tf_op jit(solution)/shard_map/reshape | solution.py:312
  71.6 0.0 copy-done.1
  71.6 0.1 dynamic_slice.7
  71.7 0.0 copy-done
  71.7 0.1 constant_dynamic-slice_fusion
  71.7 0.0 copy-done.2
  71.7 0.2 select_reduce_fusion
  71.9 0.1 broadcast_subtract_fusion
  72.0 0.8 %fusion = bf16[32,4,512]{2,1,0:T(4,128)(2,1)} fusion(f32[32,4,512]{2,1,0:T(4,128)S(1)} %reshape.52, f32[512]{0:T(512)S(1)} %copy-done.1, f32[32,4]{1,0:T(8,128)S(1)} %broadcast_subtract_fusion), kind=kLoop, calls=%fused_computation.1 | loop fusion | flops 196608 | bytes 395776 | tf_op jit(solution)/shard_map/convert_element_type | solution.py:312
  (2 shorter events, 0.0 us)
Async XLA Ops:
  0.0 71.7 %copy-start = (s32[256,2]{0,1:T(2,128)S(1)}, s32[256,2]{0,1:T(2,128)}, u32[]{:S(2)}) copy-start(s32[256,2]{0,1:T(2,128)} %param.10) | copy-start | bytes 6148
  0.0 71.6 %copy-start.1 = (f32[512]{0:T(512)S(1)}, f32[512]{0:T(512)}, u32[]{:S(2)}) copy-start(f32[512]{0:T(512)} %param.15) | copy-start | bytes 6148
  0.0 71.7 %copy-start.2 = (f32[200]{0:T(256)S(1)}, f32[200]{0:T(256)}, u32[]{:S(2)}) copy-start(f32[200]{0:T(256)} %param.14) | copy-start | bytes 2404

commit v2 on v1

v2 whole, which is shorter than its diff:
```python
import jax
import jax.numpy as jnp
from jax import lax
from jax.experimental import pallas as pl
from jax.experimental.pallas import tpu as pltpu
from jax.sharding import PartitionSpec as P

MESH = pl.DeviceIdType.MESH
BF = jnp.bfloat16
F32 = jnp.float32
I32 = jnp.int32
N = 8
PAIRS, ROWS, PIECE = 256, 32, 16
TILES, PART, WIDTH = 192, 24, 32
A_DEV, VIRT = 4, 512
DEPTH = PART * WIDTH
COLS = A_DEV * VIRT
PATH = DEPTH // 2
FAR = (4, 3, 5, 2, 6, 1, 7)
NEAR = (1, 7, 2, 6, 3, 5, 4)


def iota(shape, axis):
    return lax.broadcasted_iota(I32, shape, axis)


def hot(mask):
    return jnp.where(mask, 1.0, 0.0).astype(BF)


def dot(a, b):
    return jnp.dot(a, b, preferred_element_type=F32)


def own_slots(tiles, owner):
    place = iota((1, TILES), 1).astype(F32)
    held = (tiles >> 6) == owner
    found, last = [], None
    for _ in range(3):
        open_ = held if last is None else held & (place > last)
        last = jnp.min(jnp.where(open_, place, 999.0), axis=1, keepdims=True)
        found.append(last)
    return found


def by_slot(values, shape, axis):
    slot = iota(shape, axis) >> 5
    return jnp.where(slot == 0, values[0], jnp.where(slot == 1, values[1], values[2]))


def kernel(
    amp_in, integ, slab_in, pairs_in, virr_in, oirr_in, venergy_in, oenergy_in, out,
    amp, slab, pairs, virr, oirr, venergy, oenergy,
    vraw, vr, xs, xa, perm, spread, psb, tsym, inverse, xmine, xgive, xoth,
    ps, pr, qs, qr, sy, pf, rs, rr,
    lsem, xsem, csem, psem, qsem, gsem, hsem, rsem,
):
    v = lax.axis_index("vpair")
    x = lax.axis_index("opair")
    y, z, c = v // 16, (v // 2) % N, v % 2

    def at_x(d):
        return {"vpair": v, "opair": (x + d) % N}

    def at_y(d):
        return {"vpair": (((y + d) % N) * N + z) * 2 + c, "opair": x}

    def at_z(d):
        return {"vpair": (y * N + (z + d) % N) * 2 + c, "opair": x}

    other = {"vpair": (y * N + z) * 2 + (1 - c), "opair": x}
    steps = range(1, N)
    outer, outer_at = (z, y), (at_z, at_y)
    inner, inner_at = (y, z), (at_y, at_z)
    pending = []

    def send(src, dst, sems, i, device):
        copy = pltpu.make_async_remote_copy(
            src_ref=src, dst_ref=dst, send_sem=sems.at[0, i], recv_sem=sems.at[1, i],
            device_id=device, device_id_type=MESH,
        )
        copy.start()
        pending.append(copy)
        return copy

    loads = []
    for i, (src, dst) in enumerate((
        (amp_in, amp), (slab_in, slab), (pairs_in, pairs), (virr_in, virr), (oirr_in, oirr),
        (venergy_in, venergy), (oenergy_in, oenergy), (integ, vraw),
    )):
        loads.append(pltpu.make_async_copy(src, dst, lsem.at[i]))
        loads[-1].start()
    barrier = pltpu.get_barrier_semaphore()
    for device in [f(d) for f in (at_x, at_y, at_z) for d in steps] + [other]:
        pl.semaphore_signal(barrier, inc=1, device_id=device, device_id_type=MESH)
    loads[1].wait()

    tiles = slab[...]
    c_of, d_of = tiles >> 4, tiles & 15
    pick = hot(iota((VIRT, TILES), 0) == jnp.where(d_of == v // 8, c_of, -1))
    found = own_slots(tiles, v)
    place = iota((1, TILES), 1).astype(F32)
    ids = [
        jnp.sum(jnp.where(place == k, tiles.astype(F32), 0.0), axis=1, keepdims=True) for k in found
    ]
    tile = by_slot(ids, (1, 128), 1).astype(I32)
    wide = iota((1, 128), 1) & 31
    pick_own = hot(iota((VIRT, 128), 0) == (tile & 15) * WIDTH + wide)
    loads[0].wait()
    block = amp[...].reshape(ROWS * A_DEV, VIRT)
    lane = iota((1, N * 128), 1)
    target = jnp.where((lane & 31) < PART, (lane >> 7) * PART + (lane & 31), -1)
    place_in = hot(iota((TILES, N * 128), 0) == target)
    row = iota((ROWS * A_DEV, 1), 0) & 3
    columns = dot(dot(block, pick).astype(BF), place_in)
    columns = jnp.where(row == ((lane >> 5) & 3), columns, 0.0).astype(BF)
    held = jnp.where(row == ((tile >> 4) & 3), dot(block, pick_own), 0.0).astype(BF)
    fold = hot((iota((ROWS, ROWS * A_DEV), 1) >> 2) == iota((ROWS, ROWS * A_DEV), 0))
    columns = dot(fold, columns).astype(BF)
    held = dot(fold, held).astype(BF)
    for o in range(N):
        xs[o, :, 0:128] = held
        xs[o, :, 128:256] = columns[:, o * 128 : (o + 1) * 128]
    pl.semaphore_wait(barrier, 3 * (N - 1) + 1)

    to_x = [send(xs.at[(x + d) % N], xa.at[x], xsem, d, at_x(d)) for d in FAR]
    xa[pl.ds(x, 1)] = xs[pl.ds(x, 1)]

    for i in range(2, 7):
        loads[i].wait()
    lists = pairs[...]
    first, second = lists[0:1, :], lists[1:2, :]
    code = first * 256 + second
    swapped = jnp.broadcast_to((second * 256 + first).astype(F32), (PAIRS, PAIRS)).T
    perm[...] = hot(swapped == code.astype(F32))
    part_lane = iota((1, DEPTH), 1)
    for h in range(2):
        holder = (y * N + z) * 2 + h
        slots = [k - (x * PART).astype(F32) for k in own_slots(tiles, holder)]
        r = iota((128, 1), 0)
        slot_at = by_slot(slots, (128, 1), 0).astype(I32)
        slot_at = jnp.where(r < 96, slot_at, -1)
        spread[h, 0:128] = hot(
            (slot_at == (part_lane >> 5)) & ((r & 31) == (part_lane & 31))
        )
        spread[h, 128:256] = hot(
            ((r & 31) == (part_lane >> 5))
            & ((holder % N) * A_DEV + (r >> 5) == (part_lane & 31))
        )
    irrep_hot = hot(iota((oirr.shape[1], PAIRS), 0) == first)
    irrep_hot2 = hot(iota((oirr.shape[1], PAIRS), 0) == second)
    occ = jnp.broadcast_to(oirr[...].astype(F32), (8, oirr.shape[1])).astype(BF)
    pair_sym = dot(occ, irrep_hot).astype(I32) ^ dot(occ, irrep_hot2).astype(I32)
    psb[...] = jnp.broadcast_to(pair_sym[0:1].astype(F32), (128, PAIRS)).T
    occ = jnp.broadcast_to(oenergy[...], (8, oirr.shape[1]))
    energy = sum(
        jnp.dot(
            occ, jnp.where(iota((oirr.shape[1], PAIRS), 0) == which, 1.0, 0.0),
            precision=lax.Precision.HIGHEST, preferred_element_type=F32,
        )
        for which in (first, second)
    )
    turned = jnp.broadcast_to(energy[0:1], (128, PAIRS)).T
    inverse[:, 0:128] = turned[0:ROWS]
    for o in steps:
        inverse[:, 0:128] = jnp.where(x == o, turned[o * ROWS : (o + 1) * ROWS], inverse[:, 0:128])
    pair_energy = inverse[:, 0:1]
    vir_row = venergy[...]
    vir_lane = iota((1, VIRT), 1)
    for a in range(A_DEV):
        own_virtual = jnp.sum(
            jnp.where(vir_lane == v * A_DEV + a, vir_row, 0.0), axis=1, keepdims=True
        )
        inverse[:, a * VIRT : (a + 1) * VIRT] = 1.0 / (pair_energy - own_virtual - vir_row)
    own_hot = hot(iota((TILES, DEPTH), 0) == x * PART + (part_lane >> 5))

    def own(row_values):
        wide_values = jnp.broadcast_to(row_values.astype(F32), (8, row_values.shape[1])).astype(BF)
        return dot(wide_values, own_hot)[0:1].astype(I32)

    c_row = own(c_of >> 2) * 4 + own(c_of & 3)
    d_row = own(d_of) * WIDTH + (part_lane & 31)
    vir = jnp.broadcast_to(virr[...].astype(F32), (8, VIRT)).astype(BF)
    tile_sym = [
        dot(vir, hot(iota((VIRT, DEPTH), 0) == rows))[0:1].astype(I32) for rows in (c_row, d_row)
    ]
    tsym[...] = jnp.broadcast_to((tile_sym[0] ^ tile_sym[1]).astype(F32), (8, DEPTH))

    ri, ci = iota((128, 128), 0), iota((128, 128), 1)
    regroup = hot(((ri >> 5) == (ci & 3)) & ((ri & 31) == (ci >> 2)))

    def relayout(k, _):
        rows = dot(regroup, vraw[k].reshape(WIDTH * A_DEV, VIRT)).astype(BF)
        at = pl.ds(pl.multiple_of(k * WIDTH, WIDTH), WIDTH)
        for a in range(A_DEV):
            vr[a, at, :] = rows[a * WIDTH : (a + 1) * WIDTH]
        return 0

    loads[7].wait()
    lax.fori_loop(0, 8, relayout, 0)
    for copy in to_x:
        copy.wait_recv()

    to_core = [send(xa.at[pl.ds((1 - c) * 4, 4), :, 0:128], xoth.at[0], csem, 0, other)]
    columns = xa[:, :, 128:256].reshape(PAIRS, 128)

    def mirrored(half):
        at = pl.ds(pl.multiple_of(half * 128, 128), 128)
        return dot(perm[at, :], columns).astype(BF).reshape(4, ROWS, 128)

    xgive[...] = mirrored(1 - c)
    to_core.append(send(xgive, xoth.at[1], csem, 1, other))
    xmine[0] = xa[pl.ds(c * 4, 4), :, 0:128]
    xmine[1] = mirrored(c)

    def spread_out(ref, h):
        rows = jnp.concatenate([ref[i].reshape(128, 128) for i in range(2)], axis=1)
        return dot(rows, spread[h])

    dense = spread_out(xmine, c)
    for copy in to_core:
        copy.wait_recv()
    dense += spread_out(xoth, 1 - c)
    for p in range(2):
        ps[p] = dense[:, p * PATH : (p + 1) * PATH].astype(BF).reshape(N, PIECE, PATH)
    copies = [
        send(ps.at[p, (outer[p] + d) % N], pr.at[p, outer[p]], psem.at[p], d, outer_at[p](d))
        for d in FAR for p in range(2)
    ]
    for p in range(2):
        pr[p, pl.ds(outer[p], 1)] = ps[p, pl.ds(outer[p], 1)]
    lax.fori_loop(8, 16, relayout, 0)
    for copy in copies:
        copy.wait_recv()
    for p in range(2):
        total = pr[p, 0].astype(F32)
        for i in steps:
            total += pr[p, i].astype(F32)
        qs[p] = total.astype(BF)
    copies = [
        send(qs.at[p], qr.at[p, inner[p]], qsem.at[p], d, inner_at[p](d))
        for d in FAR for p in range(2)
    ]
    for p in range(2):
        qr[p, pl.ds(inner[p], 1)] = qs[p].reshape(1, PIECE, PATH)
    lax.fori_loop(16, 24, relayout, 0)
    for copy in copies:
        copy.wait_recv()
    mine = [c * N + outer[p] for p in range(2)]
    for p in range(2):
        total = qr[p, 0].astype(F32)
        for i in steps:
            total += qr[p, i].astype(F32)
        sym_of = psb[pl.ds(pl.multiple_of(mine[p] * PIECE, PIECE), PIECE), :][:, 0:1]
        total = jnp.where(sym_of == tsym[0:1, p * PATH : (p + 1) * PATH], total, 0.0)
        sy[p, pl.ds(mine[p], 1)] = total.astype(BF).reshape(1, PIECE, PATH)
    gathered = {
        (p, d): send(sy.at[p, mine[p]], sy.at[p, mine[p]], gsem.at[p], d, outer_at[p](d))
        for d in FAR for p in range(2)
    }
    to_other = [
        send(sy.at[p, mine[p]], sy.at[p, mine[p]], hsem.at[p], 0, other) for p in range(2)
    ]
    for d in NEAR:
        for p in range(2):
            gathered[p, d].wait_recv()
            got = c * N + (outer[p] + N - d) % N
            to_other.append(send(sy.at[p, got], sy.at[p, got], hsem.at[p], d, other))
    for copy in to_other:
        copy.wait_recv()

    ring = {}

    def pass_on(way, i, q, got):
        distance = 4 - i if i < 4 else 7 - i
        d = distance if way == 0 else N - distance
        half = 0 if (way == 0) == (i < 4) else PIECE
        value = pf[d, half : half + PIECE, q * 1024 : (q + 1) * 1024]
        if got is not None:
            value += rr[way, got, q].astype(F32)
        rs[way, i, q] = value.astype(BF)
        ring[way, i, q] = send(
            rs.at[way, i, q], rr.at[way, i, q], rsem.at[way, q], i, at_x(1 if way == 0 else N - 1)
        )

    def multiply(blocks, first):
        rows = jnp.concatenate(
            [
                jnp.concatenate(
                    [sy[p, pl.ds(((x + d) % N) * 2, 2)].reshape(ROWS, PATH) for p in range(2)],
                    axis=1,
                )
                for d in blocks
            ],
            axis=0,
        )
        for a in range(A_DEV):
            sums = dot(rows, vr[a])
            for i, d in enumerate(blocks):
                pf[d, :, a * VIRT : (a + 1) * VIRT] = sums[i * ROWS : (i + 1) * ROWS]
            if first and a % 2 == 1:
                for i in (0, 4):
                    for way in range(2):
                        pass_on(way, i, a // 2, None)

    multiply((4, 3, 5, 2), True)
    multiply((6, 1, 7, 0), False)
    for i in (0, 4, 1, 5, 2):
        for q in range(2):
            for way in range(2):
                ring[way, i, q].wait_recv()
                pass_on(way, i + 1, q, i)
    for q in range(2):
        for i in (6, 3):
            for way in range(2):
                ring[way, i, q].wait_recv()
        for half, mine_, theirs in ((0, 3, 6), (PIECE, 6, 3)):
            at = (slice(half, half + PIECE), slice(q * 1024, (q + 1) * 1024))
            total = pf[0, at[0], at[1]] + rr[0, mine_, q].astype(F32) + rr[1, theirs, q].astype(F32)
            total = total * inverse[at[0], at[1]]
            for a in range(2):
                out[at[0], 2 * q + a, :] = total[:, a * VIRT : (a + 1) * VIRT].astype(out.dtype)
    for copy in pending:
        copy.wait_send()


def local(
    amplitudes, integrals, pair_list, slab_tiles, occ_irrep, vir_irrep, occ_energy, vir_energy
):
    dma = pltpu.SemaphoreType.DMA
    occupied = occ_irrep.shape[0]
    return pl.pallas_call(
        kernel,
        out_shape=jax.ShapeDtypeStruct((ROWS, A_DEV, VIRT), F32),
        in_specs=[pl.BlockSpec(memory_space=pl.ANY)] * 8,
        out_specs=pl.BlockSpec(memory_space=pltpu.VMEM),
        scratch_shapes=[
            pltpu.VMEM((ROWS, A_DEV, VIRT), BF),
            pltpu.VMEM((1, TILES), I32),
            pltpu.VMEM((2, PAIRS), I32),
            pltpu.VMEM((1, VIRT), I32),
            pltpu.VMEM((1, occupied), I32),
            pltpu.VMEM((1, VIRT), F32),
            pltpu.VMEM((1, occupied), F32),
            pltpu.VMEM((PART, WIDTH, A_DEV, VIRT), BF),
            pltpu.VMEM((A_DEV, DEPTH, VIRT), BF),
            pltpu.VMEM((N, ROWS, 256), BF),
            pltpu.VMEM((N, ROWS, 256), BF),
            pltpu.VMEM((PAIRS, PAIRS), BF),
            pltpu.VMEM((2, 256, DEPTH), BF),
            pltpu.VMEM((PAIRS, 128), F32),
            pltpu.VMEM((8, DEPTH), F32),
            pltpu.VMEM((ROWS, COLS), F32),
            pltpu.VMEM((2, 4, ROWS, 128), BF),
            pltpu.VMEM((4, ROWS, 128), BF),
            pltpu.VMEM((2, 4, ROWS, 128), BF),
            pltpu.VMEM((2, N, PIECE, PATH), BF),
            pltpu.VMEM((2, N, PIECE, PATH), BF),
            pltpu.VMEM((2, PIECE, PATH), BF),
            pltpu.VMEM((2, N, PIECE, PATH), BF),
            pltpu.VMEM((2, 2 * N, PIECE, PATH), BF),
            pltpu.VMEM((N, ROWS, COLS), F32),
            pltpu.VMEM((2, 7, 2, PIECE, 1024), BF),
            pltpu.VMEM((2, 7, 2, PIECE, 1024), BF),
            dma((8,)),
            dma((2, N)),
            dma((2, 2)),
            dma((2, 2, N)),
            dma((2, 2, N)),
            dma((2, 2, N)),
            dma((2, 2, N)),
            dma((2, 2, 2, 7)),
        ],
        compiler_params=pltpu.CompilerParams(
            collective_id=0, has_side_effects=True, vmem_limit_bytes=60 << 20
        ),
    )(
        amplitudes,
        integrals,
        slab_tiles.reshape(1, TILES),
        pair_list.T,
        vir_irrep.reshape(1, VIRT),
        occ_irrep.reshape(1, occupied),
        vir_energy.reshape(1, VIRT),
        occ_energy.reshape(1, occupied),
    ).astype(BF)


def solution(mesh):
    in_specs = (
        P("opair", "vpair", None), P("opair", None, "vpair", None), P(), P(), P(), P(), P(), P(),
    )
    out_specs = P("opair", "vpair", None)
    return jax.shard_map(local, mesh=mesh, in_specs=in_specs, out_specs=out_specs, check_vma=False)
```

time: 73 us -> 64.2 us (0.88)
  Pallas kernels: 70.4 us -> 62.4 us
  local copies, waits for them, and re-layouts: 1.29 us -> 0 us
    pallas_call x1, Pallas kernels: 70.4 us -> 62.4 us  [local(): pl.pallas_call(kernel, out_shape=jax.ShapeDtypeStruct((ROWS, A_DEV, VIRT)...]
    reshape x1 -> x0, local copies, waits for them, and re-layouts: 1.12 us -> none  [local(): return (partial_sum.reshape(ROWS, A_DEV, VIRT) / denominator).astype(BF)]
    convert_element_type x1, other arithmetic: 0.81 us -> 1.65 us  [local(): return pl.pallas_call(kernel, out_shape=jax.ShapeDtypeStruct((ROWS, A_DEV...]
where the time goes in v2:
time: 64.2 us; the launch traced here: 64.1 us
  Pallas kernels  62.4 us (97%)
  other arithmetic  1.65 us (3%)
    pallas_call x1, Pallas kernels, local(): pl.pallas_call(kernel, out_shape=jax.ShapeDtypeStruct((ROWS, A_DEV, VIRT)...  62.4 us
    convert_element_type x1, other arithmetic, local(): return pl.pallas_call(kernel, out_shape=jax.ShapeDtypeStruct((ROWS, A_DEV...  1.65 us

profile of v2, /device:TPU:1, one launch (start us, length us, event | category | flops | bytes accessed | tf_op | source)
XLA Modules:
  0.0 64.1 jit_solution(10435738391738497012)
XLA Ops:
  0.0 62.4 %shard_map.82 = f32[32,4,512]{2,1,0:T(4,128)} custom-call(bf16[32,4,512]{2,1,0:T(4,128)(2,1)} %amp_in.1, bf16[24,32,4,512]{3,2,1,0:T(4,128)(2,1)} %integ.1, s32[1,192]{1,0:T(1,128)} %bitcast.9, s32[2,256]{1,0:T(2,128)} %bitcast.6, s32[1,512]{1,0:T(1,128)} %bitcast.7, s32[1,200]{1,0:T(1,128)} %bitcast.10, f32[1,512]{1,0:T(1,128)} %bitcast.8, f32[1,200]{1,0:T(1,128)} %bitcast.11), custom_call_target="tpu_custom_call" | custom-call | tf_op jit(solution)/shard_map/pallas_call | solution.py:332
  62.4 1.7 %convert_element_type.3 = bf16[32,4,512]{2,1,0:T(4,128)(2,1)} convert(f32[32,4,512]{2,1,0:T(4,128)} %shard_map.82) | non-fusion elementwise | flops 65536 | bytes 393216 | tf_op jit(solution)/shard_map/convert_element_type | solution.py:386

commit v3 on v2

--- a/solution.py
+++ b/solution.py
@@ -152,6 +152,139 @@
     occ = jnp.broadcast_to(oirr[...].astype(F32), (8, oirr.shape[1])).astype(BF)
     pair_sym = dot(occ, irrep_hot).astype(I32) ^ dot(occ, irrep_hot2).astype(I32)
     psb[...] = jnp.broadcast_to(pair_sym[0:1].astype(F32), (128, PAIRS)).T
+    own_hot = hot(iota((TILES, DEPTH), 0) == x * PART + (part_lane >> 5))
+
+    def own(row_values):
+        wide_values = jnp.broadcast_to(row_values.astype(F32), (8, row_values.shape[1])).astype(BF)
+        return dot(wide_values, own_hot)[0:1].astype(I32)
+
+    c_row = own(c_of >> 2) * 4 + own(c_of & 3)
+    d_row = own(d_of) * WIDTH + (part_lane & 31)
+    vir = jnp.broadcast_to(virr[...].astype(F32), (8, VIRT)).astype(BF)
+    tile_sym = [
+        dot(vir, hot(iota((VIRT, DEPTH), 0) == rows))[0:1].astype(I32) for rows in (c_row, d_row)
+    ]
+    tsym[...] = jnp.broadcast_to((tile_sym[0] ^ tile_sym[1]).astype(F32), (8, DEPTH))
+
+    ri, ci = iota((128, 128), 0), iota((128, 128), 1)
+    regroup = hot(((ri >> 5) == (ci & 3)) & ((ri & 31) == (ci >> 2)))
+
+    def relayout(k, _):
+        rows = dot(regroup, vraw[k].reshape(WIDTH * A_DEV, VIRT)).astype(BF)
+        at = pl.ds(pl.multiple_of(k * WIDTH, WIDTH), WIDTH)
+        for a in range(A_DEV):
+            vr[a, at, :] = rows[a * WIDTH : (a + 1) * WIDTH]
+        return 0
+
+    loads[7].wait()
+    for copy in to_x:
+        copy.wait_recv()
+
+    to_core = [send(xa.at[pl.ds((1 - c) * 4, 4), :, 0:128], xoth.at[0], csem, 0, other)]
+    columns = xa[:, :, 128:256].reshape(PAIRS, 128)
+
+    def mirrored(half):
+        at = pl.ds(pl.multiple_of(half * 128, 128), 128)
+        return dot(perm[at, :], columns).astype(BF).reshape(4, ROWS, 128)
+
+    xgive[...] = mirrored(1 - c)
+    to_core.append(send(xgive, xoth.at[1], csem, 1, other))
+    xmine[0] = xa[pl.ds(c * 4, 4), :, 0:128]
+    xmine[1] = mirrored(c)
+
+    def spread_out(ref, h):
+        rows = jnp.concatenate([ref[i].reshape(128, 128) for i in range(2)], axis=1)
+        return dot(rows, spread[h])
+
+    dense = spread_out(xmine, c)
+    for copy in to_core:
+        copy.wait_recv()
+    dense += spread_out(xoth, 1 - c)
+    for p in range(2):
+        ps[p] = dense[:, p * PATH : (p + 1) * PATH].astype(BF).reshape(N, PIECE, PATH)
+    copies = [
+        send(ps.at[p, (outer[p] + d) % N], pr.at[p, outer[p]], psem.at[p], d, outer_at[p](d))
+        for d in FAR for p in range(2)
+    ]
+    for p in range(2):
+        pr[p, pl.ds(outer[p], 1)] = ps[p, pl.ds(outer[p], 1)]
+    lax.fori_loop(0, 8, relayout, 0)
+    for copy in copies:
+        copy.wait_recv()
+    for p in range(2):
+        total = pr[p, 0].astype(F32)
+        for i in steps:
+            total += pr[p, i].astype(F32)
+        qs[p] = total.astype(BF)
+    copies = [
+        send(qs.at[p], qr.at[p, inner[p]], qsem.at[p], d, inner_at[p](d))
+        for d in FAR for p in range(2)
+    ]
+    for p in range(2):
+        qr[p, pl.ds(inner[p], 1)] = qs[p].reshape(1, PIECE, PATH)
+    lax.fori_loop(8, 16, relayout, 0)
+    for copy in copies:
+        copy.wait_recv()
+    mine = [c * N + outer[p] for p in range(2)]
+    for p in range(2):
+        total = qr[p, 0].astype(F32)
+        for i in steps:
+            total += qr[p, i].astype(F32)
+        sym_of = psb[pl.ds(pl.multiple_of(mine[p] * PIECE, PIECE), PIECE), :][:, 0:1]
+        total = jnp.where(sym_of == tsym[0:1, p * PATH : (p + 1) * PATH], total, 0.0)
+        sy[p, pl.ds(mine[p], 1)] = total.astype(BF).reshape(1, PIECE, PATH)
+    gathered = {
+        (p, d): send(sy.at[p, mine[p]], sy.at[p, mine[p]], gsem.at[p], d, outer_at[p](d))
+        for d in FAR for p in range(2)
+    }
+    to_other = [
+        send(sy.at[p, mine[p]], sy.at[p, mine[p]], hsem.at[p], 0, other) for p in range(2)
+    ]
+    lax.fori_loop(16, 24, relayout, 0)
+    for d in NEAR:
+        for p in range(2):
+            gathered[p, d].wait_recv()
+            got = c * N + (outer[p] + N - d) % N
+            to_other.append(send(sy.at[p, got], sy.at[p, got], hsem.at[p], d, other))
+    for copy in to_other:
+        copy.wait_recv()
+
+    ring = {}
+
+    def pass_on(way, i, q, got):
+        distance = 4 - i if i < 4 else 7 - i
+        d = distance if way == 0 else N - distance
+        half = 0 if (way == 0) == (i < 4) else PIECE
+        value = pf[d, half : half + PIECE, q * VIRT : (q + 1) * VIRT]
+        if got is not None:
+            value += rr[way, got, q].astype(F32)
+        rs[way, i, q] = value.astype(BF)
+        ring[way, i, q] = send(
+            rs.at[way, i, q], rr.at[way, i, q], rsem.at[way, q], i, at_x(1 if way == 0 else N - 1)
+        )
+
+    def multiply(blocks, first):
+        rows = jnp.concatenate(
+            [
+                jnp.concatenate(
+                    [sy[p, pl.ds(((x + d) % N) * 2, 2)].reshape(ROWS, PATH) for p in range(2)],
+                    axis=1,
+                )
+                for d in blocks
+            ],
+            axis=0,
+        )
+        for a in range(A_DEV):
+            sums = dot(rows, vr[a])
+            for i, d in enumerate(blocks):
+                pf[d, :, a * VIRT : (a + 1) * VIRT] = sums[i * ROWS : (i + 1) * ROWS]
+            if first:
+                for i in (0, 4):
+                    for way in range(2):
+                        pass_on(way, i, a, None)
+
+    multiply((4, 3, 5, 2), True)
+    multiply((6, 1, 7, 0), False)
     occ = jnp.broadcast_to(oenergy[...], (8, oirr.shape[1]))
     energy = sum(
         jnp.dot(
@@ -172,154 +305,20 @@
             jnp.where(vir_lane == v * A_DEV + a, vir_row, 0.0), axis=1, keepdims=True
         )
         inverse[:, a * VIRT : (a + 1) * VIRT] = 1.0 / (pair_energy - own_virtual - vir_row)
-    own_hot = hot(iota((TILES, DEPTH), 0) == x * PART + (part_lane >> 5))
-
-    def own(row_values):
-        wide_values = jnp.broadcast_to(row_values.astype(F32), (8, row_values.shape[1])).astype(BF)
-        return dot(wide_values, own_hot)[0:1].astype(I32)
-
-    c_row = own(c_of >> 2) * 4 + own(c_of & 3)
-    d_row = own(d_of) * WIDTH + (part_lane & 31)
-    vir = jnp.broadcast_to(virr[...].astype(F32), (8, VIRT)).astype(BF)
-    tile_sym = [
-        dot(vir, hot(iota((VIRT, DEPTH), 0) == rows))[0:1].astype(I32) for rows in (c_row, d_row)
-    ]
-    tsym[...] = jnp.broadcast_to((tile_sym[0] ^ tile_sym[1]).astype(F32), (8, DEPTH))
-
-    ri, ci = iota((128, 128), 0), iota((128, 128), 1)
-    regroup = hot(((ri >> 5) == (ci & 3)) & ((ri & 31) == (ci >> 2)))
-
-    def relayout(k, _):
-        rows = dot(regroup, vraw[k].reshape(WIDTH * A_DEV, VIRT)).astype(BF)
-        at = pl.ds(pl.multiple_of(k * WIDTH, WIDTH), WIDTH)
-        for a in range(A_DEV):
-            vr[a, at, :] = rows[a * WIDTH : (a + 1) * WIDTH]
-        return 0
-
-    loads[7].wait()
-    lax.fori_loop(0, 8, relayout, 0)
-    for copy in to_x:
-        copy.wait_recv()
-
-    to_core = [send(xa.at[pl.ds((1 - c) * 4, 4), :, 0:128], xoth.at[0], csem, 0, other)]
-    columns = xa[:, :, 128:256].reshape(PAIRS, 128)
-
-    def mirrored(half):
-        at = pl.ds(pl.multiple_of(half * 128, 128), 128)
-        return dot(perm[at, :], columns).astype(BF).reshape(4, ROWS, 128)
-
-    xgive[...] = mirrored(1 - c)
-    to_core.append(send(xgive, xoth.at[1], csem, 1, other))
-    xmine[0] = xa[pl.ds(c * 4, 4), :, 0:128]
-    xmine[1] = mirrored(c)
-
-    def spread_out(ref, h):
-        rows = jnp.concatenate([ref[i].reshape(128, 128) for i in range(2)], axis=1)
-        return dot(rows, spread[h])
-
-    dense = spread_out(xmine, c)
-    for copy in to_core:
-        copy.wait_recv()
-    dense += spread_out(xoth, 1 - c)
-    for p in range(2):
-        ps[p] = dense[:, p * PATH : (p + 1) * PATH].astype(BF).reshape(N, PIECE, PATH)
-    copies = [
-        send(ps.at[p, (outer[p] + d) % N], pr.at[p, outer[p]], psem.at[p], d, outer_at[p](d))
-        for d in FAR for p in range(2)
-    ]
-    for p in range(2):
-        pr[p, pl.ds(outer[p], 1)] = ps[p, pl.ds(outer[p], 1)]
-    lax.fori_loop(8, 16, relayout, 0)
-    for copy in copies:
-        copy.wait_recv()
-    for p in range(2):
-        total = pr[p, 0].astype(F32)
-        for i in steps:
-            total += pr[p, i].astype(F32)
-        qs[p] = total.astype(BF)
-    copies = [
-        send(qs.at[p], qr.at[p, inner[p]], qsem.at[p], d, inner_at[p](d))
-        for d in FAR for p in range(2)
-    ]
-    for p in range(2):
-        qr[p, pl.ds(inner[p], 1)] = qs[p].reshape(1, PIECE, PATH)
-    lax.fori_loop(16, 24, relayout, 0)
-    for copy in copies:
-        copy.wait_recv()
-    mine = [c * N + outer[p] for p in range(2)]
-    for p in range(2):
-        total = qr[p, 0].astype(F32)
-        for i in steps:
-            total += qr[p, i].astype(F32)
-        sym_of = psb[pl.ds(pl.multiple_of(mine[p] * PIECE, PIECE), PIECE), :][:, 0:1]
-        total = jnp.where(sym_of == tsym[0:1, p * PATH : (p + 1) * PATH], total, 0.0)
-        sy[p, pl.ds(mine[p], 1)] = total.astype(BF).reshape(1, PIECE, PATH)
-    gathered = {
-        (p, d): send(sy.at[p, mine[p]], sy.at[p, mine[p]], gsem.at[p], d, outer_at[p](d))
-        for d in FAR for p in range(2)
-    }
-    to_other = [
-        send(sy.at[p, mine[p]], sy.at[p, mine[p]], hsem.at[p], 0, other) for p in range(2)
-    ]
-    for d in NEAR:
-        for p in range(2):
-            gathered[p, d].wait_recv()
-            got = c * N + (outer[p] + N - d) % N
-            to_other.append(send(sy.at[p, got], sy.at[p, got], hsem.at[p], d, other))
-    for copy in to_other:
-        copy.wait_recv()
-
-    ring = {}
-
-    def pass_on(way, i, q, got):
-        distance = 4 - i if i < 4 else 7 - i
-        d = distance if way == 0 else N - distance
-        half = 0 if (way == 0) == (i < 4) else PIECE
-        value = pf[d, half : half + PIECE, q * 1024 : (q + 1) * 1024]
-        if got is not None:
-            value += rr[way, got, q].astype(F32)
-        rs[way, i, q] = value.astype(BF)
-        ring[way, i, q] = send(
-            rs.at[way, i, q], rr.at[way, i, q], rsem.at[way, q], i, at_x(1 if way == 0 else N - 1)
-        )
-
-    def multiply(blocks, first):
-        rows = jnp.concatenate(
-            [
-                jnp.concatenate(
-                    [sy[p, pl.ds(((x + d) % N) * 2, 2)].reshape(ROWS, PATH) for p in range(2)],
-                    axis=1,
-                )
-                for d in blocks
-            ],
-            axis=0,
-        )
-        for a in range(A_DEV):
-            sums = dot(rows, vr[a])
-            for i, d in enumerate(blocks):
-                pf[d, :, a * VIRT : (a + 1) * VIRT] = sums[i * ROWS : (i + 1) * ROWS]
-            if first and a % 2 == 1:
-                for i in (0, 4):
-                    for way in range(2):
-                        pass_on(way, i, a // 2, None)
-
-    multiply((4, 3, 5, 2), True)
-    multiply((6, 1, 7, 0), False)
     for i in (0, 4, 1, 5, 2):
-        for q in range(2):
+        for q in range(4):
             for way in range(2):
                 ring[way, i, q].wait_recv()
                 pass_on(way, i + 1, q, i)
-    for q in range(2):
+    for q in range(4):
         for i in (6, 3):
             for way in range(2):
                 ring[way, i, q].wait_recv()
         for half, mine_, theirs in ((0, 3, 6), (PIECE, 6, 3)):
-            at = (slice(half, half + PIECE), slice(q * 1024, (q + 1) * 1024))
+            at = (slice(half, half + PIECE), slice(q * VIRT, (q + 1) * VIRT))
             total = pf[0, at[0], at[1]] + rr[0, mine_, q].astype(F32) + rr[1, theirs, q].astype(F32)
             total = total * inverse[at[0], at[1]]
-            for a in range(2):
-                out[at[0], 2 * q + a, :] = total[:, a * VIRT : (a + 1) * VIRT].astype(out.dtype)
+            out[at[0], q, :] = total.astype(out.dtype)
     for copy in pending:
         copy.wait_send()
 
@@ -331,7 +330,7 @@
     occupied = occ_irrep.shape[0]
     return pl.pallas_call(
         kernel,
-        out_shape=jax.ShapeDtypeStruct((ROWS, A_DEV, VIRT), F32),
+        out_shape=jax.ShapeDtypeStruct((ROWS, A_DEV, VIRT), BF),
         in_specs=[pl.BlockSpec(memory_space=pl.ANY)] * 8,
         out_specs=pl.BlockSpec(memory_space=pltpu.VMEM),
         scratch_shapes=[
@@ -360,8 +359,8 @@
             pltpu.VMEM((2, N, PIECE, PATH), BF),
             pltpu.VMEM((2, 2 * N, PIECE, PATH), BF),
             pltpu.VMEM((N, ROWS, COLS), F32),
-            pltpu.VMEM((2, 7, 2, PIECE, 1024), BF),
-            pltpu.VMEM((2, 7, 2, PIECE, 1024), BF),
+            pltpu.VMEM((2, 7, 4, PIECE, VIRT), BF),
+            pltpu.VMEM((2, 7, 4, PIECE, VIRT), BF),
             dma((8,)),
             dma((2, N)),
             dma((2, 2)),
@@ -369,7 +368,7 @@
             dma((2, 2, N)),
             dma((2, 2, N)),
             dma((2, 2, N)),
-            dma((2, 2, 2, 7)),
+            dma((2, 4, 2, 7)),
         ],
         compiler_params=pltpu.CompilerParams(
             collective_id=0, has_side_effects=True, vmem_limit_bytes=60 << 20
@@ -383,7 +382,7 @@
         occ_irrep.reshape(1, occupied),
         vir_energy.reshape(1, VIRT),
         occ_energy.reshape(1, occupied),
-    ).astype(BF)
+    )
 
 
 def solution(mesh):

time: 64.2 us -> 64.2 us (level)
  other arithmetic: 1.65 us -> 0 us
  local copies, waits for them, and re-layouts: 0 us -> 1.61 us
    convert_element_type x1 -> x0, other arithmetic: 1.65 us -> none  [local(): return pl.pallas_call(kernel, out_shape=jax.ShapeDtypeStruct((ROWS, A_DEV...]
    unnamed x0 -> x1, local copies, waits for them, and re-layouts: none -> 1.61 us
where the time goes in v3:
time: 64.2 us; the launch traced here: 64.1 us
  Pallas kernels  62.4 us (97%)
  local copies, waits for them, and re-layouts  1.61 us (3%)
    pallas_call x1, Pallas kernels, local(): pl.pallas_call(kernel, out_shape=jax.ShapeDtypeStruct((ROWS, A_DEV, VIRT)...  62.4 us
    unnamed x1, local copies, waits for them, and re-layouts  1.61 us

profile of v3, /device:TPU:1, one launch (start us, length us, event | category | flops | bytes accessed | tf_op | source)
XLA Modules:
  0.0 64.1 jit_solution(1218298453033451865)
XLA Ops:
  0.0 62.4 %shard_map.82 = bf16[32,4,512]{2,1,0:T(4,128)(2,1)} custom-call(bf16[32,4,512]{2,1,0:T(4,128)(2,1)} %amp_in.1, bf16[24,32,4,512]{3,2,1,0:T(4,128)(2,1)} %integ.1, s32[1,192]{1,0:T(1,128)} %bitcast.9, s32[2,256]{1,0:T(2,128)} %bitcast.6, s32[1,512]{1,0:T(1,128)} %bitcast.7, s32[1,200]{1,0:T(1,128)} %bitcast.10, f32[1,512]{1,0:T(1,128)} %bitcast.8, ...), custom_call_target="tpu_custom_call" | custom-call | tf_op jit(solution)/shard_map/pallas_call | solution.py:331
  62.5 1.6 %copy.10 = bf16[32,4,512]{2,1,0:T(4,128)(2,1)} copy(bf16[32,4,512]{2,1,0:T(4,128)(2,1)} %shard_map.82) | data formatting | bytes 262144

commit v4 on v2

--- a/solution.py
+++ b/solution.py
@@ -152,6 +152,63 @@
     occ = jnp.broadcast_to(oirr[...].astype(F32), (8, oirr.shape[1])).astype(BF)
     pair_sym = dot(occ, irrep_hot).astype(I32) ^ dot(occ, irrep_hot2).astype(I32)
     psb[...] = jnp.broadcast_to(pair_sym[0:1].astype(F32), (128, PAIRS)).T
+    own_hot = hot(iota((TILES, DEPTH), 0) == x * PART + (part_lane >> 5))
+
+    def own(row_values):
+        wide_values = jnp.broadcast_to(row_values.astype(F32), (8, row_values.shape[1])).astype(BF)
+        return dot(wide_values, own_hot)[0:1].astype(I32)
+
+    c_row = own(c_of >> 2) * 4 + own(c_of & 3)
+    d_row = own(d_of) * WIDTH + (part_lane & 31)
+    vir = jnp.broadcast_to(virr[...].astype(F32), (8, VIRT)).astype(BF)
+    tile_sym = [
+        dot(vir, hot(iota((VIRT, DEPTH), 0) == rows))[0:1].astype(I32) for rows in (c_row, d_row)
+    ]
+    tsym[...] = jnp.broadcast_to((tile_sym[0] ^ tile_sym[1]).astype(F32), (8, DEPTH))
+
+    ri, ci = iota((128, 128), 0), iota((128, 128), 1)
+    regroup = hot(((ri >> 5) == (ci & 3)) & ((ri & 31) == (ci >> 2)))
+
+    def relayout(k, _):
+        rows = dot(regroup, vraw[k].reshape(WIDTH * A_DEV, VIRT)).astype(BF)
+        at = pl.ds(pl.multiple_of(k * WIDTH, WIDTH), WIDTH)
+        for a in range(A_DEV):
+            vr[a, at, :] = rows[a * WIDTH : (a + 1) * WIDTH]
+        return 0
+
+    loads[7].wait()
+    for copy in to_x:
+        copy.wait_recv()
+
+    to_core = [send(xa.at[pl.ds((1 - c) * 4, 4), :, 0:128], xoth.at[0], csem, 0, other)]
+    columns = xa[:, :, 128:256].reshape(PAIRS, 128)
+
+    def mirrored(half):
+        at = pl.ds(pl.multiple_of(half * 128, 128), 128)
+        return dot(perm[at, :], columns).astype(BF).reshape(4, ROWS, 128)
+
+    xgive[...] = mirrored(1 - c)
+    to_core.append(send(xgive, xoth.at[1], csem, 1, other))
+    xmine[0] = xa[pl.ds(c * 4, 4), :, 0:128]
+    xmine[1] = mirrored(c)
+
+    def spread_out(ref, h):
+        rows = jnp.concatenate([ref[i].reshape(128, 128) for i in range(2)], axis=1)
+        return dot(rows, spread[h])
+
+    dense = spread_out(xmine, c)
+    for copy in to_core:
+        copy.wait_recv()
+    dense += spread_out(xoth, 1 - c)
+    for p in range(2):
+        ps[p] = dense[:, p * PATH : (p + 1) * PATH].astype(BF).reshape(N, PIECE, PATH)
+    copies = [
+        send(ps.at[p, (outer[p] + d) % N], pr.at[p, outer[p]], psem.at[p], d, outer_at[p](d))
+        for d in FAR for p in range(2)
+    ]
+    for p in range(2):
+        pr[p, pl.ds(outer[p], 1)] = ps[p, pl.ds(outer[p], 1)]
+    lax.fori_loop(0, 10, relayout, 0)
     occ = jnp.broadcast_to(oenergy[...], (8, oirr.shape[1]))
     energy = sum(
         jnp.dot(
@@ -172,64 +229,6 @@
             jnp.where(vir_lane == v * A_DEV + a, vir_row, 0.0), axis=1, keepdims=True
         )
         inverse[:, a * VIRT : (a + 1) * VIRT] = 1.0 / (pair_energy - own_virtual - vir_row)
-    own_hot = hot(iota((TILES, DEPTH), 0) == x * PART + (part_lane >> 5))
-
-    def own(row_values):
-        wide_values = jnp.broadcast_to(row_values.astype(F32), (8, row_values.shape[1])).astype(BF)
-        return dot(wide_values, own_hot)[0:1].astype(I32)
-
-    c_row = own(c_of >> 2) * 4 + own(c_of & 3)
-    d_row = own(d_of) * WIDTH + (part_lane & 31)
-    vir = jnp.broadcast_to(virr[...].astype(F32), (8, VIRT)).astype(BF)
-    tile_sym = [
-        dot(vir, hot(iota((VIRT, DEPTH), 0) == rows))[0:1].astype(I32) for rows in (c_row, d_row)
-    ]
-    tsym[...] = jnp.broadcast_to((tile_sym[0] ^ tile_sym[1]).astype(F32), (8, DEPTH))
-
-    ri, ci = iota((128, 128), 0), iota((128, 128), 1)
-    regroup = hot(((ri >> 5) == (ci & 3)) & ((ri & 31) == (ci >> 2)))
-
-    def relayout(k, _):
-        rows = dot(regroup, vraw[k].reshape(WIDTH * A_DEV, VIRT)).astype(BF)
-        at = pl.ds(pl.multiple_of(k * WIDTH, WIDTH), WIDTH)
-        for a in range(A_DEV):
-            vr[a, at, :] = rows[a * WIDTH : (a + 1) * WIDTH]
-        return 0
-
-    loads[7].wait()
-    lax.fori_loop(0, 8, relayout, 0)
-    for copy in to_x:
-        copy.wait_recv()
-
-    to_core = [send(xa.at[pl.ds((1 - c) * 4, 4), :, 0:128], xoth.at[0], csem, 0, other)]
-    columns = xa[:, :, 128:256].reshape(PAIRS, 128)
-
-    def mirrored(half):
-        at = pl.ds(pl.multiple_of(half * 128, 128), 128)
-        return dot(perm[at, :], columns).astype(BF).reshape(4, ROWS, 128)
-
-    xgive[...] = mirrored(1 - c)
-    to_core.append(send(xgive, xoth.at[1], csem, 1, other))
-    xmine[0] = xa[pl.ds(c * 4, 4), :, 0:128]
-    xmine[1] = mirrored(c)
-
-    def spread_out(ref, h):
-        rows = jnp.concatenate([ref[i].reshape(128, 128) for i in range(2)], axis=1)
-        return dot(rows, spread[h])
-
-    dense = spread_out(xmine, c)
-    for copy in to_core:
-        copy.wait_recv()
-    dense += spread_out(xoth, 1 - c)
-    for p in range(2):
-        ps[p] = dense[:, p * PATH : (p + 1) * PATH].astype(BF).reshape(N, PIECE, PATH)
-    copies = [
-        send(ps.at[p, (outer[p] + d) % N], pr.at[p, outer[p]], psem.at[p], d, outer_at[p](d))
-        for d in FAR for p in range(2)
-    ]
-    for p in range(2):
-        pr[p, pl.ds(outer[p], 1)] = ps[p, pl.ds(outer[p], 1)]
-    lax.fori_loop(8, 16, relayout, 0)
     for copy in copies:
         copy.wait_recv()
     for p in range(2):
@@ -243,7 +242,7 @@
     ]
     for p in range(2):
         qr[p, pl.ds(inner[p], 1)] = qs[p].reshape(1, PIECE, PATH)
-    lax.fori_loop(16, 24, relayout, 0)
+    lax.fori_loop(10, 24, relayout, 0)
     for copy in copies:
         copy.wait_recv()
     mine = [c * N + outer[p] for p in range(2)]
@@ -258,14 +257,12 @@
         (p, d): send(sy.at[p, mine[p]], sy.at[p, mine[p]], gsem.at[p], d, outer_at[p](d))
         for d in FAR for p in range(2)
     }
-    to_other = [
-        send(sy.at[p, mine[p]], sy.at[p, mine[p]], hsem.at[p], 0, other) for p in range(2)
-    ]
-    for d in NEAR:
-        for p in range(2):
+    half = pl.ds(c * N, N)
+    to_other = []
+    for p in range(2):
+        for d in NEAR:
             gathered[p, d].wait_recv()
-            got = c * N + (outer[p] + N - d) % N
-            to_other.append(send(sy.at[p, got], sy.at[p, got], hsem.at[p], d, other))
+        to_other.append(send(sy.at[p, half], sy.at[p, half], hsem, p, other))
     for copy in to_other:
         copy.wait_recv()
 
@@ -275,7 +272,7 @@
         distance = 4 - i if i < 4 else 7 - i
         d = distance if way == 0 else N - distance
         half = 0 if (way == 0) == (i < 4) else PIECE
-        value = pf[d, half : half + PIECE, q * 1024 : (q + 1) * 1024]
+        value = pf[d, half : half + PIECE, q * VIRT : (q + 1) * VIRT]
         if got is not None:
             value += rr[way, got, q].astype(F32)
         rs[way, i, q] = value.astype(BF)
@@ -283,7 +280,7 @@
             rs.at[way, i, q], rr.at[way, i, q], rsem.at[way, q], i, at_x(1 if way == 0 else N - 1)
         )
 
-    def multiply(blocks, first):
+    def multiply(blocks):
         rows = jnp.concatenate(
             [
                 jnp.concatenate(
@@ -298,28 +295,25 @@
             sums = dot(rows, vr[a])
             for i, d in enumerate(blocks):
                 pf[d, :, a * VIRT : (a + 1) * VIRT] = sums[i * ROWS : (i + 1) * ROWS]
-            if first and a % 2 == 1:
-                for i in (0, 4):
-                    for way in range(2):
-                        pass_on(way, i, a // 2, None)
-
-    multiply((4, 3, 5, 2), True)
-    multiply((6, 1, 7, 0), False)
+            for i in (0, 4):
+                for way in range(2):
+                    pass_on(way, i, a, None)
+
+    multiply((4, 3, 5, 2, 6, 1, 7, 0))
     for i in (0, 4, 1, 5, 2):
-        for q in range(2):
+        for q in range(4):
             for way in range(2):
                 ring[way, i, q].wait_recv()
                 pass_on(way, i + 1, q, i)
-    for q in range(2):
+    for q in range(4):
         for i in (6, 3):
             for way in range(2):
                 ring[way, i, q].wait_recv()
         for half, mine_, theirs in ((0, 3, 6), (PIECE, 6, 3)):
-            at = (slice(half, half + PIECE), slice(q * 1024, (q + 1) * 1024))
+            at = (slice(half, half + PIECE), slice(q * VIRT, (q + 1) * VIRT))
             total = pf[0, at[0], at[1]] + rr[0, mine_, q].astype(F32) + rr[1, theirs, q].astype(F32)
             total = total * inverse[at[0], at[1]]
-            for a in range(2):
-                out[at[0], 2 * q + a, :] = total[:, a * VIRT : (a + 1) * VIRT].astype(out.dtype)
+            out[at[0], q, :] = total.astype(out.dtype)
     for copy in pending:
         copy.wait_send()
 
@@ -331,7 +325,7 @@
     occupied = occ_irrep.shape[0]
     return pl.pallas_call(
         kernel,
-        out_shape=jax.ShapeDtypeStruct((ROWS, A_DEV, VIRT), F32),
+        out_shape=jax.ShapeDtypeStruct((ROWS, A_DEV, VIRT), BF),
         in_specs=[pl.BlockSpec(memory_space=pl.ANY)] * 8,
         out_specs=pl.BlockSpec(memory_space=pltpu.VMEM),
         scratch_shapes=[
@@ -360,16 +354,16 @@
             pltpu.VMEM((2, N, PIECE, PATH), BF),
             pltpu.VMEM((2, 2 * N, PIECE, PATH), BF),
             pltpu.VMEM((N, ROWS, COLS), F32),
-            pltpu.VMEM((2, 7, 2, PIECE, 1024), BF),
-            pltpu.VMEM((2, 7, 2, PIECE, 1024), BF),
+            pltpu.VMEM((2, 7, 4, PIECE, VIRT), BF),
+            pltpu.VMEM((2, 7, 4, PIECE, VIRT), BF),
             dma((8,)),
             dma((2, N)),
             dma((2, 2)),
             dma((2, 2, N)),
             dma((2, 2, N)),
             dma((2, 2, N)),
-            dma((2, 2, N)),
-            dma((2, 2, 2, 7)),
+            dma((2, 2)),
+            dma((2, 4, 2, 7)),
         ],
         compiler_params=pltpu.CompilerParams(
             collective_id=0, has_side_effects=True, vmem_limit_bytes=60 << 20
@@ -383,7 +377,7 @@
         occ_irrep.reshape(1, occupied),
         vir_energy.reshape(1, VIRT),
         occ_energy.reshape(1, occupied),
-    ).astype(BF)
+    )
 
 
 def solution(mesh):

time: 64.2 us -> 64.3 us (level)
  other arithmetic: 1.65 us -> 0 us
  local copies, waits for them, and re-layouts: 0 us -> 1.61 us
    convert_element_type x1 -> x0, other arithmetic: 1.65 us -> none  [local(): return pl.pallas_call(kernel, out_shape=jax.ShapeDtypeStruct((ROWS, A_DEV...]
    unnamed x0 -> x1, local copies, waits for them, and re-layouts: none -> 1.61 us
where the time goes in v4:
time: 64.3 us; the launch traced here: 64.2 us
  Pallas kernels  62.6 us (97%)
  local copies, waits for them, and re-layouts  1.61 us (3%)
    pallas_call x1, Pallas kernels, local(): pl.pallas_call(kernel, out_shape=jax.ShapeDtypeStruct((ROWS, A_DEV, VIRT)...  62.6 us
    unnamed x1, local copies, waits for them, and re-layouts  1.61 us

profile of v4, /device:TPU:1, one launch (start us, length us, event | category | flops | bytes accessed | tf_op | source)
XLA Modules:
  0.0 64.2 jit_solution(11571693091087489829)
XLA Ops:
  0.0 62.6 %shard_map.82 = bf16[32,4,512]{2,1,0:T(4,128)(2,1)} custom-call(bf16[32,4,512]{2,1,0:T(4,128)(2,1)} %amp_in.1, bf16[24,32,4,512]{3,2,1,0:T(4,128)(2,1)} %integ.1, s32[1,192]{1,0:T(1,128)} %bitcast.9, s32[2,256]{1,0:T(2,128)} %bitcast.6, s32[1,512]{1,0:T(1,128)} %bitcast.7, s32[1,200]{1,0:T(1,128)} %bitcast.10, f32[1,512]{1,0:T(1,128)} %bitcast.8, ...), custom_call_target="tpu_custom_call" | custom-call | tf_op jit(solution)/shard_map/pallas_call | solution.py:326
  62.6 1.6 %copy.10 = bf16[32,4,512]{2,1,0:T(4,128)(2,1)} copy(bf16[32,4,512]{2,1,0:T(4,128)(2,1)} %shard_map.82) | data formatting | bytes 262144
